TPU v7x, 512 devices: a whole 4x8x8 slice. The times are simulated.
512 devices in a mesh: role: 4 (over x), cls: 128 (over y, z, core).
Axes of the slice: x: 4, y: 8, z: 8, core: 2. Of those that a mesh axis runs over, the one named last changes fastest.
Arguments:
- features: bfloat16 [1024, 512], P('cls', 'role'), may hold values from -160 to 160, as said below
- centres: bfloat16 [1572864, 512], P(('role', 'cls')), may hold values from -0.25 to 0.25
- samples: int32 [512, 1024], P(('role', 'cls')), may hold values from 0 to 3071, as said below
- counts: int32 [512], P(('role', 'cls')), may hold values from 64 to 1024, as said below
- label_row: int32 [1024], replicated, may hold values from 0 to 3071, as said below
- owner: int32 [1024], replicated, may hold values from 0 to 511, as said below
Outputs:
- feature_grad: float32 [1024, 512], P('cls', 'role')
- centre_grad: bfloat16 [512, 1024, 512], P(('role', 'cls'))
- loss: float32 [1024], P('cls')
Inputs may be any that keep to these rules, and one draw needn't show every extreme that they name: `features`: scaled values with spread per image and per feature. `samples`: entries of one shard are distinct; only the first counts[q] entries of shard q are used. `counts`: each count is 1024 divided by 1, 2, 4, 8 or 16; some shard has exactly 1024. label_row[i] stands among the first counts[owner[i]] entries of samples[owner[i]]. `owner`: index of the owning shard along role+cls; shards with more used slots own more images.
All inputs are finite; a program needn't handle non-finite values.
Results may differ from a plain program's by a relative error of at most 0.0061.
Values may be sent and summed in bfloat16 or wider, within the bound.
A program may use at most 64 MiB of HBM per device.

v0:
```python
import math
import jax
import jax.numpy as jnp
from jax import lax
from jax.sharding import PartitionSpec as P

logit_scale = 64.0
margin_cos = math.cos(0.5)
margin_sin = math.sin(0.5)
epsilon = 1e-05


def body(features, centres, samples, counts, label_row, owner):
    cls_size = lax.axis_size("cls")
    img_rows = features.shape[0]
    images = img_rows * cls_size
    values = features.astype(jnp.float32)
    col_mean = lax.psum(jnp.sum(values, 0), "cls") / images
    centred = values - col_mean
    col_var = lax.psum(jnp.sum(centred * centred, 0), "cls") / images
    inv_std = lax.rsqrt(col_var + epsilon)
    normed = centred * inv_std
    norm_sq = lax.psum(jnp.sum(normed * normed, 1), "role")
    inv_norm = lax.rsqrt(norm_sq + epsilon)
    unit_feats = normed * inv_norm[:, None]
    widened = lax.all_gather(unit_feats.astype(jnp.bfloat16), "role", axis=1, tiled=True)
    gathered = lax.all_gather(widened, "cls", axis=0, tiled=True)
    shard_id = lax.axis_index("role") * cls_size + lax.axis_index("cls")
    row_ids = samples[0]
    live_count = counts[0]
    picked = jnp.take(centres, row_ids, axis=0).astype(jnp.float32)
    w_inv = lax.rsqrt(jnp.sum(picked * picked, 1) + epsilon)
    w_unit = picked * w_inv[:, None]
    w_round = w_unit.astype(jnp.bfloat16)
    cosine = lax.dot_general(
        gathered, w_round, (((1,), (1,)), ((), ())), preferred_element_type=jnp.float32
    )
    slot_ids = jnp.arange(row_ids.shape[0], dtype=jnp.int32)
    usable = slot_ids < live_count
    positive = (
        (owner[:, None] == shard_id) & (label_row[:, None] == row_ids[None, :]) & usable[None, :]
    )
    sine_part = jnp.sqrt(jnp.maximum(1.0 - cosine * cosine, 0.0))
    target = cosine * margin_cos - sine_part * margin_sin
    logits = logit_scale * jnp.where(positive, target, cosine)
    exp_terms = jnp.where(usable[None, :], jnp.exp(logits), jnp.float32(0.0))
    part_sum = jnp.sum(exp_terms, 1)
    part_pos = jnp.sum(jnp.where(positive, logits, jnp.float32(0.0)), 1)
    partition_sum, positive_logit = lax.psum((part_sum, part_pos), ("role", "cls"))
    loss_all = jnp.log(partition_sum) - positive_logit
    loss = lax.dynamic_slice_in_dim(loss_all, lax.axis_index("cls") * img_rows, img_rows, 0)
    grad_logit = logit_scale * (exp_terms / partition_sum[:, None] - positive.astype(jnp.float32))
    grad_round = grad_logit.astype(jnp.bfloat16)
    back_rows = lax.dot_general(
        grad_round, gathered, (((0,), (0,)), ((), ())), preferred_element_type=jnp.float32
    )
    radial_rows = jnp.sum(w_unit * back_rows, 1, keepdims=True)
    centre_grad = ((back_rows - w_unit * radial_rows) * w_inv[:, None]).astype(jnp.bfloat16)[None]
    full_grad = jnp.dot(grad_round, w_round, preferred_element_type=jnp.float32)
    split_grad = lax.psum_scatter(full_grad, "role", scatter_dimension=1, tiled=True)
    grad_unit = lax.psum_scatter(split_grad, "cls", scatter_dimension=0, tiled=True)
    radial_part = lax.psum(jnp.sum(unit_feats * grad_unit, 1), "role")
    grad_normed = (grad_unit - unit_feats * radial_part[:, None]) * inv_norm[:, None]
    grad_total, cross_total = lax.psum(
        (jnp.sum(grad_normed, 0), jnp.sum(grad_normed * normed, 0)), "cls"
    )
    feature_grad = (grad_normed - grad_total / images - normed * (cross_total / images)) * inv_std
    return (feature_grad, centre_grad, loss)


def solution(mesh):
    return jax.shard_map(
        body,
        mesh=mesh,
        in_specs=(
            P("cls", "role"),
            P(("role", "cls"), None),
            P(("role", "cls"), None),
            P(("role", "cls")),
            P(),
            P(),
        ),
        out_specs=(P("cls", "role"), P(("role", "cls"), None, None), P("cls")),
        check_vma=False,
    )
```

profile of v0, /device:TPU:1, one launch (start us, length us, event | category | flops | bytes accessed | tf_op | source)
XLA Modules:
  0.0 1212.5 jit_solution(9806286267377754459)
XLA Ops:
  7.2 0.0 copy-start
  7.2 0.0 all-gather.2.cloned.1.call-start
  7.2 0.8 convert_reduce_fusion
  8.1 254.6 %psum.56 = f32[128]{0:T(128)S(1)} all-reduce(f32[128]{0:T(128)S(1)} %convert_reduce_fusion), channel_id=1, replica_groups=mesh['role'=4,'cls'=128] {'cls'}, use_global_device_ids=true, to_apply=%region_1.0 | all-reduce | flops 128 | bytes 1024 | tf_op jit(solution)/shard_map/psum | solution.py:18
  262.7 0.7 fusion.31
  263.4 251.2 %psum.57 = f32[128]{0:T(128)S(1)} all-reduce(f32[128]{0:T(128)S(1)} %fusion.31), channel_id=1, replica_groups=mesh['role'=4,'cls'=128] {'cls'}, use_global_device_ids=true, to_apply=%region_3.0 | all-reduce | flops 128 | bytes 1024 | tf_op jit(solution)/shard_map/psum | solution.py:20
  514.6 0.8 fusion.27
  515.4 8.5 psum.58
  523.9 0.8 fusion.23
  524.6 8.4 all_gather.6
  533.1 0.0 all-gather.2.cloned.1.call-update
  533.1 0.0 reduce-scatter.2.cloned.1.call-start
  533.1 0.7 compare_select_fusion
  533.8 0.0 copy-done
  533.8 0.0 copy-start.4
  533.9 0.0 copy-start.6
  533.9 5.1 gather_fusion
  539.0 0.0 copy-start.5
  539.0 2.3 copy.13
  541.9 0.0 copy-done.4
  541.9 0.0 copy-done.6
  542.0 1.5 fusion.8
  543.5 66.5 %all-gather.2.cloned.1.call-done = bf16[1024,512]{1,0:T(8,128)(2,1)} async-done(((bf16[8,512]{1,0:T(8,128)(2,1)}), bf16[1024,512]{1,0:T(8,128)(2,1)}) %all-gather.2.cloned.1.call-update) | async-done | bytes 1048592 | tf_op jit(solution)/shard_map/all_gather | solution.py:27
  610.0 0.0 copy-done.5
  610.0 7.4 select_reduce_fusion
  617.4 96.5 %all-reduce.1 = (f32[1024]{0:T(1024)S(1)}, f32[1024]{0:T(1024)S(1)}) all-reduce(f32[1024]{0:T(1024)S(1)} %get-tuple-element.13, f32[1024]{0:T(1024)S(1)} %get-tuple-element.12), channel_id=1, replica_groups=mesh['role'=4,'cls'=128] {'role','cls'}, use_global_device_ids=true, to_apply=%region_8.9 | all-reduce | flops 2048 | bytes 16384 | tf_op jit(solution)/shard_map/psum | solution.py:49
  713.9 3.5 multiply_convert_fusion
  717.4 0.0 copy-start.2
  717.4 1.3 copy-done.2
  718.8 0.0 copy-done.1
  718.8 2.6 fusion.10
  721.4 0.0 reduce-scatter.2.cloned.1.call-update
  721.4 0.0 all-reduce.5.cloned.1.call-start
  721.4 1.3 dynamic-slice
  723.4 4.8 fusion.4
  728.2 22.0 %reduce-scatter.2.cloned.1.call-done = f32[1024,128]{1,0:T(8,128)} async-done(((f32[1024,512]{1,0:T(8,128)}), f32[1024,128]{1,0:T(8,128)}) %reduce-scatter.2.cloned.1.call-update) | async-done | bytes 524304 | tf_op jit(solution)/shard_map/reduce_scatter | solution.py:60
  750.2 0.0 all-reduce.5.cloned.1.call-update
  750.2 0.0 copy-start.3
  750.2 3.3 fusion.9
  753.5 2.3 copy.14
  755.8 188.5 %all-reduce.5.cloned.1.call-done = f32[1024,128]{1,0:T(8,128)} async-done(((f32[1024,128]{1,0:T(8,128)}), f32[1024,128]{1,0:T(8,128)}) %all-reduce.5.cloned.1.call-update) | async-done | bytes 524304
  944.3 0.0 copy-done.3
  944.3 0.9 fusion.24
  945.2 0.6 dynamic_slice.3
  945.8 8.4 psum.60
  954.1 0.8 fusion.34
  954.9 249.7 %all-reduce.2 = (f32[128]{0:T(128)S(1)}, f32[128]{0:T(128)S(1)}) all-reduce(f32[128]{0:T(128)S(1)} %get-tuple-element.15, f32[128]{0:T(128)S(1)} %get-tuple-element.14), channel_id=1, replica_groups=mesh['role'=4,'cls'=128] {'cls'}, use_global_device_ids=true, to_apply=%region_16.17 | all-reduce | flops 256 | bytes 2048 | tf_op jit(solution)/shard_map/psum | solution.py:64
  1204.6 1.4 fusion.30
  (11 shorter events, 0.1 us)
Async XLA Ops:
  7.2 526.7 %copy-start = (bf16[3072,512]{1,0:T(8,128)(2,1)S(1)}, bf16[3072,512]{1,0:T(8,128)(2,1)}, u32[]{:S(2)}) copy-start(bf16[3072,512]{1,0:T(8,128)(2,1)} %param.7) | copy-start | bytes 9437188
  7.2 602.8 %all-gather.2.cloned.1.call-start = ((), (), s32[]{:S(2)}) async-start(), calls=%async_computation.1 | async-start | bytes 1056768 | tf_op jit(solution)/shard_map/all_gather | solution.py:27
  533.1 217.1 %reduce-scatter.2.cloned.1.call-start = ((), (), s32[]{:S(2)}) async-start(), calls=%async_computation.2 | async-start | bytes 2621440 | tf_op jit(solution)/shard_map/reduce_scatter | solution.py:60
  533.8 8.1 copy-start.4
  533.9 8.1 copy-start.6
  539.0 71.0 %copy-start.5 = (s32[1024]{0:T(1024)S(1)}, s32[1024]{0:T(1024)}, u32[]{:S(2)}) copy-start(s32[1024]{0:T(1024)} %param.10) | copy-start | bytes 12292
  713.9 4.9 copy-start.1
  717.4 1.3 copy-start.2
  721.4 222.9 %all-reduce.5.cloned.1.call-start = ((), (), s32[]{:S(2)}) async-start(), calls=%async_computation.3 | async-start | bytes 1048576
  750.2 194.1 %copy-start.3 = (bf16[8,128]{1,0:T(8,128)(2,1)S(1)}, bf16[8,128]{1,0:T(8,128)(2,1)}, u32[]{:S(2)}) copy-start(bf16[8,128]{1,0:T(8,128)(2,1)} %param.6) | copy-start | bytes 6148
Sparse Core Ops, SparseCore 0:
  533.2 76.7 all-gather.1
  721.5 28.6 reduce-scatter.1
  753.7 190.5 all-reduce.4
where the time goes:
time: 1210 us
  blocking collectives  877 us (72%)
  waiting for transfers between devices  277 us (23%)
  other arithmetic  15.3 us (1%)
  between operations  15.2 us (1%)
  matrix products  14.8 us (1%)
  local copies, waits for them, and re-layouts  12.9 us (1%)
    psum x1, blocking collectives, body(): col_mean = lax.psum(jnp.sum(values, 0), 'cls') / images  255 us
    psum x1, blocking collectives, body(): col_var = lax.psum(jnp.sum(centred * centred, 0), 'cls') / images  251 us
    psum x1, blocking collectives, body(): lax.psum((jnp.sum(grad_normed, 0), jnp.sum(grad_normed * normed, 0)), 'cls')  250 us
    unnamed x4, waiting for transfers between devices  189 us
    psum x1, blocking collectives, body(): lax.psum((part_sum, part_pos), ('role', 'cls'))  96.5 us
    all_gather x1, waiting for transfers between devices, body(): gathered = lax.all_gather(widened, 'cls', axis=0, tiled=True)  66.5 us
  transfers between devices with their start and end apart: 3, of which 3 were waited for; matrix products, arithmetic and copies ran while one was open for 2% of the time, Pallas kernels for 0%

commit v1 on v0

--- a/solution.py
+++ b/solution.py
@@ -8,6 +8,11 @@
 margin_cos = math.cos(0.5)
 margin_sin = math.sin(0.5)
 epsilon = 1e-05
+
+
+def _connect_column(matrix, mesh_ax, a_name):
+    found_now = jax.lax.psum(jax.lax.psum(matrix, mesh_ax), a_name)
+    return found_now
 
 
 def body(features, centres, samples, counts, label_row, owner):
@@ -46,7 +51,7 @@
     exp_terms = jnp.where(usable[None, :], jnp.exp(logits), jnp.float32(0.0))
     part_sum = jnp.sum(exp_terms, 1)
     part_pos = jnp.sum(jnp.where(positive, logits, jnp.float32(0.0)), 1)
-    partition_sum, positive_logit = lax.psum((part_sum, part_pos), ("role", "cls"))
+    partition_sum, positive_logit = _connect_column((part_sum, part_pos), "cls", "role")
     loss_all = jnp.log(partition_sum) - positive_logit
     loss = lax.dynamic_slice_in_dim(loss_all, lax.axis_index("cls") * img_rows, img_rows, 0)
     grad_logit = logit_scale * (exp_terms / partition_sum[:, None] - positive.astype(jnp.float32))

time: 1210 us -> 1390 us (1.15)
  blocking collectives: 877 us -> 1050 us
    psum x1 -> x3, blocking collectives: 96.5 us -> 261 us  [_connect_column(): found_now = jax.lax.psum(jax.lax.psum(matrix, mesh_ax), a_name)]
  transfers between devices with their start and end apart: 3 -> 3, of which waited for: 3 -> 3; matrix products, arithmetic and copies ran while one was open for 2% -> 1% of each run, Pallas kernels for 0% -> 0%
where the time goes in v1:
time: 1390 us
  blocking collectives  1050 us (76%)
  waiting for transfers between devices  282 us (20%)
  other arithmetic  15.3 us (1%)
  between operations  15.2 us (1%)
  matrix products  14.8 us (1%)
    psum x3, blocking collectives, _connect_column(): found_now = jax.lax.psum(jax.lax.psum(matrix, mesh_ax), a_name)  261 us
    psum x1, blocking collectives, body(): col_mean = lax.psum(jnp.sum(values, 0), 'cls') / images  255 us
    psum x1, blocking collectives, body(): lax.psum((jnp.sum(grad_normed, 0), jnp.sum(grad_normed * normed, 0)), 'cls')  254 us
    psum x1, blocking collectives, body(): col_var = lax.psum(jnp.sum(centred * centred, 0), 'cls') / images  251 us
    unnamed x4, waiting for transfers between devices  191 us
    all_gather x1, waiting for transfers between devices, body(): gathered = lax.all_gather(widened, 'cls', axis=0, tiled=True)  66.5 us
  transfers between devices with their start and end apart: 3, of which 3 were waited for; matrix products, arithmetic and copies ran while one was open for 1% of the time, Pallas kernels for 0%

profile of v1, /device:TPU:1, one launch (start us, length us, event | category | flops | bytes accessed | tf_op | source)
XLA Modules:
  0.0 1386.0 jit_solution(1073263015068995166)
XLA Ops:
  7.2 0.0 copy-start
  7.2 0.0 all-gather.2.cloned.1.call-start
  7.2 0.8 convert_reduce_fusion
  8.1 254.6 %psum.70 = f32[128]{0:T(128)S(1)} all-reduce(f32[128]{0:T(128)S(1)} %convert_reduce_fusion), channel_id=1, replica_groups=mesh['role'=4,'cls'=128] {'cls'}, use_global_device_ids=true, to_apply=%region_1.0 | all-reduce | flops 128 | bytes 1024 | tf_op jit(solution)/shard_map/psum | solution.py:23
  262.7 0.7 fusion.31
  263.4 251.2 %psum.71 = f32[128]{0:T(128)S(1)} all-reduce(f32[128]{0:T(128)S(1)} %fusion.31), channel_id=1, replica_groups=mesh['role'=4,'cls'=128] {'cls'}, use_global_device_ids=true, to_apply=%region_3.0 | all-reduce | flops 128 | bytes 1024 | tf_op jit(solution)/shard_map/psum | solution.py:25
  514.6 0.8 fusion.27
  515.4 8.5 psum.72
  523.9 0.8 fusion.23
  524.6 8.4 all_gather.6
  533.1 0.0 all-gather.2.cloned.1.call-update
  533.1 0.0 reduce-scatter.2.cloned.1.call-start
  533.1 0.7 compare_select_fusion
  533.8 0.0 copy-done
  533.8 0.0 copy-start.4
  533.9 0.0 copy-start.6
  533.9 5.1 gather_fusion
  539.0 2.3 copy.13
  541.9 0.0 copy-done.4
  541.9 0.0 copy-done.6
  542.0 1.5 fusion.8
  543.5 66.5 %all-gather.2.cloned.1.call-done = bf16[1024,512]{1,0:T(8,128)(2,1)} async-done(((bf16[8,512]{1,0:T(8,128)(2,1)}), bf16[1024,512]{1,0:T(8,128)(2,1)}) %all-gather.2.cloned.1.call-update) | async-done | bytes 1048592 | tf_op jit(solution)/shard_map/all_gather | solution.py:32
  610.0 0.0 copy-done.5
  610.0 7.4 select_reduce_fusion
  617.4 246.4 %psum.73 = f32[1024]{0:T(1024)S(1)} all-reduce(f32[1024]{0:T(1024)S(1)} %get-tuple-element.13), channel_id=1, replica_groups=mesh['role'=4,'cls'=128] {'cls'}, use_global_device_ids=true, to_apply=%region_8.9 | all-reduce | flops 1024 | bytes 8192 | tf_op jit(solution)/shard_map/psum | solution.py:14
  863.8 8.4 psum.74
  872.2 3.5 multiply_convert_fusion
  875.7 0.0 copy-start.2
  875.8 1.3 copy-done.2
  877.1 0.0 copy-done.1
  877.1 2.6 fusion.10
  879.7 0.0 reduce-scatter.2.cloned.1.call-update
  879.7 0.0 all-reduce.4.cloned.1.call-start
  879.7 1.3 dynamic-slice
  881.7 4.8 fusion.4
  886.5 24.7 %reduce-scatter.2.cloned.1.call-done = f32[1024,128]{1,0:T(8,128)} async-done(((f32[1024,512]{1,0:T(8,128)}), f32[1024,128]{1,0:T(8,128)}) %reduce-scatter.2.cloned.1.call-update) | async-done | bytes 524304 | tf_op jit(solution)/shard_map/reduce_scatter | solution.py:65
  911.2 0.0 all-reduce.4.cloned.1.call-update
  911.2 3.3 fusion.9
  914.5 190.9 %all-reduce.4.cloned.1.call-done = f32[1024,128]{1,0:T(8,128)} async-done(((f32[1024,128]{1,0:T(8,128)}), f32[1024,128]{1,0:T(8,128)}) %all-reduce.4.cloned.1.call-update) | async-done | bytes 524304
  1105.4 0.0 copy-done.3
  1105.4 0.9 fusion.24
  1106.3 2.3 copy.14
  1108.6 8.4 psum.75
  1117.0 0.8 fusion.34
  1117.7 253.7 %all-reduce.1 = (f32[128]{0:T(128)S(1)}, f32[128]{0:T(128)S(1)}, f32[1024]{0:T(1024)S(1)}) all-reduce(f32[128]{0:T(128)S(1)} %get-tuple-element.15, f32[128]{0:T(128)S(1)} %get-tuple-element.14, f32[1024]{0:T(1024)S(1)} %get-tuple-element.12), channel_id=1, replica_groups=mesh['role'=4,'cls'=128] {'cls'}, use_global_device_ids=true, to_apply=%region_17.18 | all-reduce | flops 1280 | bytes 10240 | tf_op jit(solution)/shard_map/psum | solution.py:69
  1371.5 6.0 psum.79
  1377.5 0.6 dynamic_slice.3
  1378.1 1.4 fusion.30
  (13 shorter events, 0.1 us)
Async XLA Ops:
  7.2 526.7 %copy-start = (bf16[3072,512]{1,0:T(8,128)(2,1)S(1)}, bf16[3072,512]{1,0:T(8,128)(2,1)}, u32[]{:S(2)}) copy-start(bf16[3072,512]{1,0:T(8,128)(2,1)} %param.7) | copy-start | bytes 9437188
  7.2 602.8 %all-gather.2.cloned.1.call-start = ((), (), s32[]{:S(2)}) async-start(), calls=%async_computation.1 | async-start | bytes 1056768 | tf_op jit(solution)/shard_map/all_gather | solution.py:32
  533.1 378.1 %reduce-scatter.2.cloned.1.call-start = ((), (), s32[]{:S(2)}) async-start(), calls=%async_computation.2 | async-start | bytes 2621440 | tf_op jit(solution)/shard_map/reduce_scatter | solution.py:65
  533.8 8.1 copy-start.4
  533.9 8.1 copy-start.6
  539.0 71.0 %copy-start.5 = (s32[1024]{0:T(1024)S(1)}, s32[1024]{0:T(1024)}, u32[]{:S(2)}) copy-start(s32[1024]{0:T(1024)} %param.10) | copy-start | bytes 12292
  872.2 4.9 copy-start.1
  875.7 1.3 copy-start.2
  879.7 225.7 %all-reduce.4.cloned.1.call-start = ((), (), s32[]{:S(2)}) async-start(), calls=%async_computation.3 | async-start | bytes 1048576
  886.5 218.9 %copy-start.3 = (bf16[8,128]{1,0:T(8,128)(2,1)S(1)}, bf16[8,128]{1,0:T(8,128)(2,1)}, u32[]{:S(2)}) copy-start(bf16[8,128]{1,0:T(8,128)(2,1)} %param.6) | copy-start | bytes 6148
Sparse Core Ops, SparseCore 0:
  533.2 76.7 all-gather.1
  879.8 31.3 reduce-scatter.1
  914.8 190.6 all-reduce.3

commit v2 on v0

--- a/solution.py
+++ b/solution.py
@@ -1,3 +1,4 @@
+import functools
 import math
 import jax
 import jax.numpy as jnp
@@ -10,12 +11,19 @@
 epsilon = 1e-05
 
 
+def carry_cells(packet, net_axis):
+    return lax.all_gather(packet, net_axis).sum(axis=0)
+
+
+settle_sheet = functools.partial(carry_cells, net_axis="cls")
+
+
 def body(features, centres, samples, counts, label_row, owner):
     cls_size = lax.axis_size("cls")
     img_rows = features.shape[0]
     images = img_rows * cls_size
     values = features.astype(jnp.float32)
-    col_mean = lax.psum(jnp.sum(values, 0), "cls") / images
+    col_mean = settle_sheet(jnp.sum(values, 0)) / images
     centred = values - col_mean
     col_var = lax.psum(jnp.sum(centred * centred, 0), "cls") / images
     inv_std = lax.rsqrt(col_var + epsilon)

time: 1210 us -> 1010 us (0.83)
  blocking collectives: 877 us -> 670 us
    psum x1 -> x0, blocking collectives: 255 us -> none  [body(): col_mean = lax.psum(jnp.sum(values, 0), 'cls') / images]
    all_gather x0 -> x1, blocking collectives: none -> 52 us  [carry_cells(): return lax.all_gather(packet, net_axis).sum(axis=0)]
where the time goes in v2:
time: 1010 us
  blocking collectives  670 us (66%)
  waiting for transfers between devices  281 us (28%)
  other arithmetic  15.4 us (2%)
  between operations  15.2 us (2%)
  matrix products  14.8 us (1%)
  local copies, waits for them, and re-layouts  12.9 us (1%)
    psum x1, blocking collectives, body(): lax.psum((jnp.sum(grad_normed, 0), jnp.sum(grad_normed * normed, 0)), 'cls')  250 us
    psum x1, blocking collectives, body(): col_var = lax.psum(jnp.sum(centred * centred, 0), 'cls') / images  246 us
    unnamed x4, waiting for transfers between devices  189 us
    psum x1, blocking collectives, body(): lax.psum((part_sum, part_pos), ('role', 'cls'))  96.5 us
    all_gather x1, waiting for transfers between devices, body(): gathered = lax.all_gather(widened, 'cls', axis=0, tiled=True)  69.9 us
    all_gather x1, blocking collectives, carry_cells(): return lax.all_gather(packet, net_axis).sum(axis=0)  52 us
    reduce_scatter x1, waiting for transfers between devices, body(): lax.psum_scatter(full_grad, 'role', scatter_dimension=1, tiled=True)  22 us
  transfers between devices with their start and end apart: 3, of which 3 were waited for; matrix products, arithmetic and copies ran while one was open for 2% of the time, Pallas kernels for 0%

profile of v2, /device:TPU:1, one launch (start us, length us, event | category | flops | bytes accessed | tf_op | source)
XLA Modules:
  0.0 1008.7 jit_solution(10704165766303852030)
XLA Ops:
  7.2 0.0 copy-start
  7.2 0.0 all-gather.4.cloned.1.call-start
  7.2 0.8 convert_reduce_fusion
  8.1 52.0 %all-gather.1 = f32[128,1,128]{2,1,0:T(1,128)S(1)} all-gather(f32[1,1,128]{2,1,0:T(1,128)S(1)} %bitcast.18), channel_id=2, replica_groups=mesh['role'=4,'cls'=128] {'cls'}, dimensions={0}, use_global_device_ids=true | all-gather | bytes 66048 | tf_op jit(solution)/shard_map/all_gather | solution.py:15
  60.0 0.2 reduce_sum.100
  60.2 0.7 fusion.31
  60.9 246.3 %psum.49 = f32[128]{0:T(128)S(1)} all-reduce(f32[128]{0:T(128)S(1)} %fusion.31), channel_id=1, replica_groups=mesh['role'=4,'cls'=128] {'cls'}, use_global_device_ids=true, to_apply=%region_3.0 | all-reduce | flops 128 | bytes 1024 | tf_op jit(solution)/shard_map/psum | solution.py:28
  307.2 0.8 fusion.27
  308.0 8.5 psum.50
  316.5 0.8 fusion.23
  317.3 8.4 all_gather.14
  325.7 0.0 all-gather.4.cloned.1.call-update
  325.7 0.0 reduce-scatter.2.cloned.1.call-start
  325.7 0.7 compare_select_fusion
  326.4 0.0 copy-done
  326.5 0.0 copy-start.4
  326.5 0.0 copy-start.6
  326.5 5.1 gather_fusion
  331.6 2.3 copy.13
  334.5 0.0 copy-done.4
  334.5 0.0 copy-done.6
  334.6 1.5 fusion.8
  336.1 69.9 %all-gather.4.cloned.1.call-done = bf16[1024,512]{1,0:T(8,128)(2,1)} async-done(((bf16[8,512]{1,0:T(8,128)(2,1)}), bf16[1024,512]{1,0:T(8,128)(2,1)}) %all-gather.4.cloned.1.call-update) | async-done | bytes 1048592 | tf_op jit(solution)/shard_map/all_gather | solution.py:35
  406.0 0.0 copy-done.5
  406.0 7.4 select_reduce_fusion
  413.4 96.5 %all-reduce.1 = (f32[1024]{0:T(1024)S(1)}, f32[1024]{0:T(1024)S(1)}) all-reduce(f32[1024]{0:T(1024)S(1)} %get-tuple-element.13, f32[1024]{0:T(1024)S(1)} %get-tuple-element.12), channel_id=1, replica_groups=mesh['role'=4,'cls'=128] {'role','cls'}, use_global_device_ids=true, to_apply=%region_8.9 | all-reduce | flops 2048 | bytes 16384 | tf_op jit(solution)/shard_map/psum | solution.py:57
  509.9 3.5 multiply_convert_fusion
  513.5 0.0 copy-start.2
  513.5 1.3 copy-done.2
  514.8 0.0 copy-done.1
  514.8 2.6 fusion.10
  517.4 0.0 reduce-scatter.2.cloned.1.call-update
  517.4 0.0 all-reduce.5.cloned.1.call-start
  517.5 1.3 dynamic-slice
  519.4 4.8 fusion.4
  524.2 22.0 %reduce-scatter.2.cloned.1.call-done = f32[1024,128]{1,0:T(8,128)} async-done(((f32[1024,512]{1,0:T(8,128)}), f32[1024,128]{1,0:T(8,128)}) %reduce-scatter.2.cloned.1.call-update) | async-done | bytes 524304 | tf_op jit(solution)/shard_map/reduce_scatter | solution.py:68
  546.2 0.0 all-reduce.5.cloned.1.call-update
  546.2 0.0 copy-start.3
  546.2 3.3 fusion.9
  549.6 2.3 copy.14
  551.8 188.7 %all-reduce.5.cloned.1.call-done = f32[1024,128]{1,0:T(8,128)} async-done(((f32[1024,128]{1,0:T(8,128)}), f32[1024,128]{1,0:T(8,128)}) %all-reduce.5.cloned.1.call-update) | async-done | bytes 524304
  740.5 0.0 copy-done.3
  740.5 0.9 fusion.24
  741.4 0.6 dynamic_slice.3
  742.0 8.4 psum.52
  750.4 0.8 fusion.34
  751.1 249.7 %all-reduce.2 = (f32[128]{0:T(128)S(1)}, f32[128]{0:T(128)S(1)}) all-reduce(f32[128]{0:T(128)S(1)} %get-tuple-element.15, f32[128]{0:T(128)S(1)} %get-tuple-element.14), channel_id=1, replica_groups=mesh['role'=4,'cls'=128] {'cls'}, use_global_device_ids=true, to_apply=%region_16.17 | all-reduce | flops 256 | bytes 2048 | tf_op jit(solution)/shard_map/psum | solution.py:72
  1000.8 1.4 fusion.30
  (12 shorter events, 0.1 us)
Async XLA Ops:
  7.2 319.3 %copy-start = (bf16[3072,512]{1,0:T(8,128)(2,1)S(1)}, bf16[3072,512]{1,0:T(8,128)(2,1)}, u32[]{:S(2)}) copy-start(bf16[3072,512]{1,0:T(8,128)(2,1)} %param.7) | copy-start | bytes 9437188
  7.2 398.8 %all-gather.4.cloned.1.call-start = ((), (), s32[]{:S(2)}) async-start(), calls=%async_computation.1 | async-start | bytes 1056768 | tf_op jit(solution)/shard_map/all_gather | solution.py:35
  325.7 220.5 %reduce-scatter.2.cloned.1.call-start = ((), (), s32[]{:S(2)}) async-start(), calls=%async_computation.2 | async-start | bytes 2621440 | tf_op jit(solution)/shard_map/reduce_scatter | solution.py:68
  326.5 8.1 copy-start.4
  326.5 8.1 copy-start.6
  331.6 74.4 %copy-start.5 = (s32[1024]{0:T(1024)S(1)}, s32[1024]{0:T(1024)}, u32[]{:S(2)}) copy-start(s32[1024]{0:T(1024)} %param.10) | copy-start | bytes 12292
  509.9 4.9 copy-start.1
  513.5 1.3 copy-start.2
  517.4 223.1 %all-reduce.5.cloned.1.call-start = ((), (), s32[]{:S(2)}) async-start(), calls=%async_computation.3 | async-start | bytes 1048576
  546.2 194.3 %copy-start.3 = (bf16[8,128]{1,0:T(8,128)(2,1)S(1)}, bf16[8,128]{1,0:T(8,128)(2,1)}, u32[]{:S(2)}) copy-start(bf16[8,128]{1,0:T(8,128)(2,1)} %param.6) | copy-start | bytes 6148
Sparse Core Ops, SparseCore 0:
  325.8 80.1 all-gather.3
  517.5 28.6 reduce-scatter.1
  549.8 190.7 all-reduce.4
